TPU v7x, 32 devices: a whole 2x2x4 slice. The times are simulated.
32 devices in a mesh: row: 4 (over y, x), col: 8 (over z, core).
Axes of the slice: x: 2, y: 2, z: 4, core: 2. Of those that a mesh axis runs over, the one named last changes fastest.
Arguments:
- incoming: float32 [4, 8, 4, 128, 128], P('row', 'col'), may hold values from -6 to 6
- block_map: int32 [4, 8, 4], P('row', 'col'), may hold values from 0 to 127, as said below
- panel_row: float32 [4, 4, 128, 16, 8, 128], P(None, 'row', None, None, 'col'), may hold values from -0.125 to 0.125
- diag_inverse: float32 [2, 8, 128, 128], P(None, 'col'), may hold values from -1 to 2.5
Outputs:
- panel_solution: float32 [128, 2, 8, 128], P('row', None, 'col')
- trailing_rhs: float32 [128, 14, 8, 128], P('row', None, 'col')
Inputs may be any that keep to these rules, and one draw needn't show every extreme that they name: block_map names every block index from 0 to 127 exactly once; the 4 blocks of one device lie in distinct grid columns, block b lying in grid column b mod 8.
All inputs are finite; a program needn't handle non-finite values.
Results may differ from a plain program's by a relative error of at most 0.00013.
Values sent between devices are 32-bit elements; how exact they have to be, the bound alone decides.
A program may use at most 64 MiB of HBM per device.

v0:
```python
import jax
import jax.numpy as jnp
from jax import lax
from jax.sharding import PartitionSpec as P


def spread(value, axis, source):
    kept = jnp.where(lax.axis_index(axis) == source, value, 0).astype(value.dtype)
    return lax.psum(kept, axis)


def take_at(array, position, axis):
    return lax.dynamic_index_in_dim(array, position, axis, keepdims=False)


def per_device(incoming, block_map, panel_row, diag_inverse):
    highest = lax.Precision.HIGHEST
    grid_rows = lax.axis_size("row")
    grid_cols = lax.axis_size("col")
    my_row = lax.axis_index("row")
    my_col = lax.axis_index("col")
    source_blocks = incoming.shape[2]
    rhs_count = incoming.shape[3]
    block_size = incoming.shape[4]
    rhs_share = rhs_count // grid_rows
    tile_rows = panel_row.shape[0]
    slot_count = panel_row.shape[3]
    tile_cols = diag_inverse.shape[0]
    panel_blocks = tile_rows * grid_rows
    targets = block_map.reshape(source_blocks)
    columns_of = (
        targets[None, :] % grid_cols == jnp.arange(grid_cols, dtype=jnp.int32)[:, None]
    ).astype(jnp.float32)
    pieces = incoming.reshape(source_blocks, grid_rows, rhs_share, block_size)
    outgoing = jnp.einsum("cu,upke->pcke", columns_of, pieces, precision=highest)
    labels = (
        jnp.einsum("cu,u->c", columns_of, (targets + 1).astype(jnp.float32), precision=highest)
        - 1.0
    )
    labels = jnp.broadcast_to(labels[None, :, None], (grid_rows, grid_cols, 1))
    received, labels_in = (
        lax.all_to_all(
            outgoing.reshape(grid_rows * grid_cols, rhs_share, block_size),
            ("row", "col"),
            split_axis=0,
            concat_axis=0,
            tiled=True,
        ),
        lax.all_to_all(
            labels.reshape(grid_rows * grid_cols, 1),
            ("row", "col"),
            split_axis=0,
            concat_axis=0,
            tiled=True,
        ),
    )
    wanted = jnp.arange(slot_count, dtype=jnp.int32) * grid_cols + my_col
    matches = (labels_in[:, 0].astype(jnp.int32)[None, :] == wanted[:, None]).astype(jnp.float32)
    local_rhs = jnp.einsum("sq,qke->kse", matches, received, precision=highest)
    local_upper = panel_row.reshape(tile_rows, block_size, slot_count, block_size)
    inverse = diag_inverse.reshape(tile_cols, block_size, block_size)
    upper_panel = panel_row[:, :, :, :tile_cols]
    gathered_upper = lax.all_gather(upper_panel, "row", axis=1, tiled=True).reshape(
        panel_blocks, block_size, tile_cols, block_size
    )

    def advance(block_index, slices):
        slot_index = block_index // grid_cols
        owner_col = block_index % grid_cols
        upper_strip = take_at(gathered_upper, slot_index, 2)
        carried = jnp.einsum("jkf,jfe->ke", slices, upper_strip, precision=highest)
        residue = take_at(local_rhs, slot_index, 1) - carried
        solved_slice = jnp.einsum(
            "kf,ef->ke", residue, take_at(inverse, slot_index, 0), precision=highest
        )
        shared = spread(solved_slice, "col", owner_col)
        return lax.dynamic_update_index_in_dim(slices, shared, block_index, 0)

    slices = lax.fori_loop(
        0, panel_blocks, advance, jnp.zeros((panel_blocks, rhs_share, block_size), jnp.float32)
    )
    solved = lax.all_gather(slices, "row", axis=1, tiled=True)
    own_share = lax.dynamic_slice_in_dim(solved, my_row * rhs_share, rhs_share, 1)
    panel_part = jnp.take(
        own_share, jnp.arange(tile_cols, dtype=jnp.int32) * grid_cols + my_col, axis=0
    )
    panel_solution = jnp.transpose(panel_part, (1, 0, 2))[:, :, None, :]
    own_rows = jnp.take(solved, jnp.arange(tile_rows, dtype=jnp.int32) * grid_rows + my_row, axis=0)
    reduced = lax.psum_scatter(
        jnp.einsum("tkf,tfse->kse", own_rows, local_upper[:, :, tile_cols:, :], precision=highest),
        "row",
        scatter_dimension=0,
        tiled=True,
    )
    trailing = local_rhs[:, tile_cols:, :] - reduced
    return (panel_solution, trailing[:, :, None, :])


def solution(mesh):
    in_specs = (
        P("row", "col", None, None, None),
        P("row", "col", None),
        P(None, "row", None, None, "col", None),
        P(None, "col", None, None),
    )
    out_specs = (P("row", None, "col", None), P("row", None, "col", None))
    return jax.shard_map(
        per_device, mesh=mesh, in_specs=in_specs, out_specs=out_specs, check_vma=False
    )
```

profile of v0, /device:TPU:0, one launch (start us, length us, event | category | flops | bytes accessed | tf_op | source)
XLA Modules:
  0.0 552.6 jit_solution(4618250720278267813)
XLA Ops:
  7.2 2.2 slice.9
  10.2 0.8 fusion.13
  11.0 0.7 broadcast_in_dim.71
  11.7 7.3 %all-to-all-start.1 = ((f32[32,1,1]{2,1,0:T(1,128)}), f32[32,1,1]{2,1,0:T(1,128)S(1)}, u32[]{:S(2)}, u32[]{:S(2)}) async-start(f32[32,1,1]{2,1,0:T(1,128)} %broadcast_in_dim.71), calls=%async_computation.1 | async-start | bytes 32768 | tf_op jit(solution)/shard_map/all_to_all | solution.py:49
  19.7 0.9 copy.28
  20.6 5.5 %all-to-all-done.1 = f32[32,1,1]{2,1,0:T(1,128)S(1)} async-done(((f32[32,1,1]{2,1,0:T(1,128)}), f32[32,1,1]{2,1,0:T(1,128)S(1)}, u32[]{:S(2)}, u32[]{:S(2)}) %all-to-all-start.1) | async-done | bytes 160 | tf_op jit(solution)/shard_map/all_to_all | solution.py:49
  26.1 2.6 all-to-all-start
  29.4 15.7 %all-to-all-done = f32[32,32,128]{2,1,0:T(8,128)S(1)} async-done(((f32[32,32,128]{2,1,0:T(8,128)}), f32[32,32,128]{2,1,0:T(8,128)S(1)}, u32[]{:S(2)}, u32[]{:S(2)}) %all-to-all-start) | async-done | bytes 524320 | tf_op jit(solution)/shard_map/all_to_all | solution.py:42
  45.8 4.6 all-gather.3.cloned.1.call-done
  50.4 1.8 copy.31
  52.2 432.0 %while.15 = (s32[]{:T(128)}, f32[16,32,128]{2,1,0:T(8,128)S(1)}, f32[32,16,128]{2,1,0:T(8,128)S(1)}, f32[16,128,2,128]{3,1,0,2:T(8,128)S(1)}, f32[2,128,128]{2,1...) while((s32[]{:T(128)}, f32[16,32,128]{2,1,0:T(8,128)S(1)}, ...), condition=%wide.region_2.3_spmd, body=%wide.region_0.2_spmd.sunk | while | flops 106967056 | bytes 1540457 | solution.py:79
  52.3 0.7 fusion.50
  53.2 28.0 %psum.15 = f32[1,32,128]{2,1,0:T(8,128)S(1)} all-reduce(f32[1,32,128]{2,1,0:T(8,128)S(1)} %fusion.51), channel_id=1, replica_groups=mesh['row'=4,'col'=8] {'col'}, use_global_device_ids=true, to_apply=%region_1.1 | all-reduce | flops 4096 | bytes 32768 | tf_op jit(solution)/shard_map/while/body/eval_jaxpr/psum | solution.py:9
  81.2 0.7 fusion.50
  82.2 25.9 %psum.15 = f32[1,32,128]{2,1,0:T(8,128)S(1)} all-reduce(f32[1,32,128]{2,1,0:T(8,128)S(1)} %fusion.51), channel_id=1, replica_groups=mesh['row'=4,'col'=8] {'col'}, use_global_device_ids=true, to_apply=%region_1.1 | all-reduce | flops 4096 | bytes 32768 | tf_op jit(solution)/shard_map/while/body/eval_jaxpr/psum | solution.py:9
  108.1 0.7 fusion.50
  109.0 25.9 %psum.15 = f32[1,32,128]{2,1,0:T(8,128)S(1)} all-reduce(f32[1,32,128]{2,1,0:T(8,128)S(1)} %fusion.51), channel_id=1, replica_groups=mesh['row'=4,'col'=8] {'col'}, use_global_device_ids=true, to_apply=%region_1.1 | all-reduce | flops 4096 | bytes 32768 | tf_op jit(solution)/shard_map/while/body/eval_jaxpr/psum | solution.py:9
  135.0 0.7 fusion.50
  135.9 25.9 %psum.15 = f32[1,32,128]{2,1,0:T(8,128)S(1)} all-reduce(f32[1,32,128]{2,1,0:T(8,128)S(1)} %fusion.51), channel_id=1, replica_groups=mesh['row'=4,'col'=8] {'col'}, use_global_device_ids=true, to_apply=%region_1.1 | all-reduce | flops 4096 | bytes 32768 | tf_op jit(solution)/shard_map/while/body/eval_jaxpr/psum | solution.py:9
  161.8 0.7 fusion.50
  162.8 25.9 %psum.15 = f32[1,32,128]{2,1,0:T(8,128)S(1)} all-reduce(f32[1,32,128]{2,1,0:T(8,128)S(1)} %fusion.51), channel_id=1, replica_groups=mesh['row'=4,'col'=8] {'col'}, use_global_device_ids=true, to_apply=%region_1.1 | all-reduce | flops 4096 | bytes 32768 | tf_op jit(solution)/shard_map/while/body/eval_jaxpr/psum | solution.py:9
  188.7 0.7 fusion.50
  189.6 25.9 %psum.15 = f32[1,32,128]{2,1,0:T(8,128)S(1)} all-reduce(f32[1,32,128]{2,1,0:T(8,128)S(1)} %fusion.51), channel_id=1, replica_groups=mesh['row'=4,'col'=8] {'col'}, use_global_device_ids=true, to_apply=%region_1.1 | all-reduce | flops 4096 | bytes 32768 | tf_op jit(solution)/shard_map/while/body/eval_jaxpr/psum | solution.py:9
  215.6 0.7 fusion.50
  216.5 25.9 %psum.15 = f32[1,32,128]{2,1,0:T(8,128)S(1)} all-reduce(f32[1,32,128]{2,1,0:T(8,128)S(1)} %fusion.51), channel_id=1, replica_groups=mesh['row'=4,'col'=8] {'col'}, use_global_device_ids=true, to_apply=%region_1.1 | all-reduce | flops 4096 | bytes 32768 | tf_op jit(solution)/shard_map/while/body/eval_jaxpr/psum | solution.py:9
  242.4 0.7 fusion.50
  243.4 25.9 %psum.15 = f32[1,32,128]{2,1,0:T(8,128)S(1)} all-reduce(f32[1,32,128]{2,1,0:T(8,128)S(1)} %fusion.51), channel_id=1, replica_groups=mesh['row'=4,'col'=8] {'col'}, use_global_device_ids=true, to_apply=%region_1.1 | all-reduce | flops 4096 | bytes 32768 | tf_op jit(solution)/shard_map/while/body/eval_jaxpr/psum | solution.py:9
  269.3 0.7 fusion.50
  270.2 25.9 %psum.15 = f32[1,32,128]{2,1,0:T(8,128)S(1)} all-reduce(f32[1,32,128]{2,1,0:T(8,128)S(1)} %fusion.51), channel_id=1, replica_groups=mesh['row'=4,'col'=8] {'col'}, use_global_device_ids=true, to_apply=%region_1.1 | all-reduce | flops 4096 | bytes 32768 | tf_op jit(solution)/shard_map/while/body/eval_jaxpr/psum | solution.py:9
  296.2 0.7 fusion.50
  297.1 25.9 %psum.15 = f32[1,32,128]{2,1,0:T(8,128)S(1)} all-reduce(f32[1,32,128]{2,1,0:T(8,128)S(1)} %fusion.51), channel_id=1, replica_groups=mesh['row'=4,'col'=8] {'col'}, use_global_device_ids=true, to_apply=%region_1.1 | all-reduce | flops 4096 | bytes 32768 | tf_op jit(solution)/shard_map/while/body/eval_jaxpr/psum | solution.py:9
  323.0 0.7 fusion.50
  324.0 25.9 %psum.15 = f32[1,32,128]{2,1,0:T(8,128)S(1)} all-reduce(f32[1,32,128]{2,1,0:T(8,128)S(1)} %fusion.51), channel_id=1, replica_groups=mesh['row'=4,'col'=8] {'col'}, use_global_device_ids=true, to_apply=%region_1.1 | all-reduce | flops 4096 | bytes 32768 | tf_op jit(solution)/shard_map/while/body/eval_jaxpr/psum | solution.py:9
  350.8 25.9 %psum.15 = f32[1,32,128]{2,1,0:T(8,128)S(1)} all-reduce(f32[1,32,128]{2,1,0:T(8,128)S(1)} %fusion.51), channel_id=1, replica_groups=mesh['row'=4,'col'=8] {'col'}, use_global_device_ids=true, to_apply=%region_1.1 | all-reduce | flops 4096 | bytes 32768 | tf_op jit(solution)/shard_map/while/body/eval_jaxpr/psum | solution.py:9
  377.7 25.9 %psum.15 = f32[1,32,128]{2,1,0:T(8,128)S(1)} all-reduce(f32[1,32,128]{2,1,0:T(8,128)S(1)} %fusion.51), channel_id=1, replica_groups=mesh['row'=4,'col'=8] {'col'}, use_global_device_ids=true, to_apply=%region_1.1 | all-reduce | flops 4096 | bytes 32768 | tf_op jit(solution)/shard_map/while/body/eval_jaxpr/psum | solution.py:9
  404.6 25.9 %psum.15 = f32[1,32,128]{2,1,0:T(8,128)S(1)} all-reduce(f32[1,32,128]{2,1,0:T(8,128)S(1)} %fusion.51), channel_id=1, replica_groups=mesh['row'=4,'col'=8] {'col'}, use_global_device_ids=true, to_apply=%region_1.1 | all-reduce | flops 4096 | bytes 32768 | tf_op jit(solution)/shard_map/while/body/eval_jaxpr/psum | solution.py:9
  431.4 25.9 %psum.15 = f32[1,32,128]{2,1,0:T(8,128)S(1)} all-reduce(f32[1,32,128]{2,1,0:T(8,128)S(1)} %fusion.51), channel_id=1, replica_groups=mesh['row'=4,'col'=8] {'col'}, use_global_device_ids=true, to_apply=%region_1.1 | all-reduce | flops 4096 | bytes 32768 | tf_op jit(solution)/shard_map/while/body/eval_jaxpr/psum | solution.py:9
  458.3 25.9 %psum.15 = f32[1,32,128]{2,1,0:T(8,128)S(1)} all-reduce(f32[1,32,128]{2,1,0:T(8,128)S(1)} %fusion.51), channel_id=1, replica_groups=mesh['row'=4,'col'=8] {'col'}, use_global_device_ids=true, to_apply=%region_1.1 | all-reduce | flops 4096 | bytes 32768 | tf_op jit(solution)/shard_map/while/body/eval_jaxpr/psum | solution.py:9
  484.2 0.7 copy-done.1
  485.0 5.5 copy.45
  490.5 18.4 %all-gather.5.cloned.1.call-done = f32[16,128,128]{2,1,0:T(8,128)} async-done(((f32[16,32,128]{2,1,0:T(8,128)}), f32[16,128,128]{2,1,0:T(8,128)}) %all-gather.5.cloned.1.call-update) | async-done | bytes 1048592 | tf_op jit(solution)/shard_map/all_gather | solution.py:82
  508.9 1.8 gather_fusion.1
  510.7 4.0 fusion.10
  514.8 1.5 copy.34
  516.3 1.0 constant_dynamic-slice_fusion.1
  518.6 25.6 %reduce-scatter.2.cloned.1.call-done = f32[32,14,128]{2,1,0:T(8,128)} async-done(((f32[128,14,128]{2,1,0:T(8,128)}), f32[32,14,128]{2,1,0:T(8,128)}) %reduce-scatter.2.cloned.1.call-update) | async-done | bytes 229392 | tf_op jit(solution)/shard_map/reduce_scatter | solution.py:89
  544.2 1.0 fusion.15
  545.2 0.9 copy.36
  (80 shorter events, 11.2 us)
Async XLA Ops:
  7.2 11.9 %copy-start = (f32[1,1,4,128,128]{4,3,2,1,0:T(8,128)S(1)}, f32[1,1,4,128,128]{4,3,2,1,0:T(8,128)}, u32[]{:S(2)}) copy-start(f32[1,1,4,128,128]{4,3,2,1,0:T(8,128)} %param.6) | copy-start | bytes 786436
  7.2 43.2 %all-gather.3.cloned.1.call-start = ((), (), s32[]{:S(2)}) async-start(), calls=%async_computation.3 | async-start | bytes 2621440 | tf_op jit(solution)/shard_map/all_gather | solution.py:63
  11.7 14.4 %all-to-all-start.1 = ((f32[32,1,1]{2,1,0:T(1,128)}), f32[32,1,1]{2,1,0:T(1,128)S(1)}, u32[]{:S(2)}, u32[]{:S(2)}) async-start(f32[32,1,1]{2,1,0:T(1,128)} %broadcast_in_dim.71), calls=%async_computation.1 | async-start | bytes 32768 | tf_op jit(solution)/shard_map/all_to_all | solution.py:49
  19.6 32.6 %copy-start.2 = (f32[2,1,128,128]{3,2,1,0:T(8,128)S(1)}, f32[2,1,128,128]{3,2,1,0:T(8,128)}, u32[]{:S(2)}) copy-start(f32[2,1,128,128]{3,2,1,0:T(8,128)} %param.9) | copy-start | bytes 393220
  26.1 19.0 %all-to-all-start = ((f32[32,32,128]{2,1,0:T(8,128)}), f32[32,32,128]{2,1,0:T(8,128)S(1)}, u32[]{:S(2)}, u32[]{:S(2)}) async-start(f32[32,32,128]{2,1,0:T(8,128)} %bitcast.11), calls=%async_computation | async-start | bytes 1048576 | tf_op jit(solution)/shard_map/all_to_all | solution.py:42
  28.7 480.2 %all-gather.5.cloned.1.call-start = ((), (), s32[]{:S(2)}) async-start(), calls=%async_computation.4 | async-start | bytes 1310720 | tf_op jit(solution)/shard_map/all_gather | solution.py:82
  484.2 0.7 copy-start.1
  485.0 59.2 %reduce-scatter.2.cloned.1.call-start = ((), (), s32[]{:S(2)}) async-start(), calls=%async_computation.5 | async-start | bytes 1310720 | tf_op jit(solution)/shard_map/reduce_scatter | solution.py:89
Sparse Core Ops, SparseCore 0:
  9.9 40.4 all-gather.2
  485.1 23.8 all-gather.4
  516.4 27.7 reduce-scatter.1
where the time goes:
time: 553 us
  blocking collectives  417 us (75%)
  waiting for transfers between devices  69.9 us (13%)
  matrix products  20.6 us (4%)
  local copies, waits for them, and re-layouts  18.7 us (3%)
  between operations  13.9 us (3%)
  starting transfers between devices  10 us (2%)
    psum x16, blocking collectives, spread(): return lax.psum(kept, axis)  417 us
    reduce_scatter x1, waiting for transfers between devices, per_device(): lax.psum_scatter(jnp.einsum('tkf,tfse->kse', own_rows, local_upper[:, :,...  25.6 us
    all_gather x1, waiting for transfers between devices, per_device(): solved = lax.all_gather(slices, 'row', axis=1, tiled=True)  18.4 us
    all_to_all x1, waiting for transfers between devices, per_device(): lax.all_to_all(outgoing.reshape(grid_rows * grid_cols, rhs_share, block_s...  15.7 us
    dot_general x16, matrix products, advance(): carried = jnp.einsum('jkf,jfe->ke', slices, upper_strip, precision=highest)  11.4 us
  transfers between devices with their start and end apart: 5, of which 5 were waited for; matrix products, arithmetic and copies ran while one was open for 2% of the time, Pallas kernels for 0%

commit v1 on v0

v1 whole, which is shorter than its diff:
```python
import functools

import jax
import jax.numpy as jnp
from jax import lax
from jax.experimental import pallas as pl
from jax.experimental.pallas import tpu as pltpu
from jax.sharding import PartitionSpec as P

MESH = pl.DeviceIdType.MESH
F32 = jnp.float32
BF16 = jnp.bfloat16


def split(x):
    high = x.astype(BF16)
    return high, (x - high.astype(F32)).astype(BF16)


def dot_split(a, b, b_dim=0):
    dims = (((1,), (b_dim,)), ((), ()))

    def one(x, y):
        return lax.dot_general(x, y, dims, preferred_element_type=F32)

    a_high, a_low = a
    b_high, b_low = b
    return one(a_high, b_high) + (one(a_low, b_high) + one(a_high, b_low))


def dot3(a, b, b_dim=0):
    return dot_split(split(a), split(b), b_dim)


def kernel(sizes, bm, inc, up, inv, sol_out, tr_out, outb, recv, g, uv, yall, acc, part, rbuf, yh, yl,
           a_send, a_recv, g_send, g_recv, u_sem, y_send, y_recv, f_send, p_send, p_recv):
    NR, NC, SB, KS, NB, TR, SLOTS, TC = sizes
    PB = TR * NR
    TS = SLOTS - TC
    N = NR * NC
    r = lax.axis_index("row")
    c = lax.axis_index("col")
    me = r * NC + c

    def remote(src, dst, ssem, rsem, row, col):
        return pltpu.make_async_remote_copy(
            src_ref=src, dst_ref=dst, send_sem=ssem, recv_sem=rsem, device_id=(row, col), device_id_type=MESH)

    barrier = pltpu.get_barrier_semaphore()

    @pl.loop(1, N)
    def _(k):
        t = lax.rem(me + k, N)
        pl.semaphore_signal(barrier, inc=1, device_id=(t // NC, lax.rem(t, NC)), device_id_type=MESH)

    for s in range(TC):
        for t in range(TR):
            a = t * NR + r

            @pl.when(a < s * NC + c)
            def _(s=s, t=t, a=a):
                pltpu.make_async_copy(up.at[t, :, s, :], g.at[a, s], g_recv.at[a, s]).start()

    @pl.loop(0, TS)
    def _(s):
        pltpu.make_async_copy(up.at[:, :, TC + s, :], uv.at[s], u_sem.at[s]).start()

    @pl.loop(0, NC)
    def _(cc):
        pick = jnp.int32(0)
        label = jnp.int32(-1)
        for u in range(SB):
            b = bm[u]
            hit = lax.rem(b, NC) == cc
            pick = jnp.where(hit, u, pick)
            label = jnp.where(hit, b, label)
        outb[cc, :, :KS, :] = inc[pick]
        outb[cc, :, KS:, :] = jnp.full((NR, 8, NB), label.astype(F32), F32)

    pl.semaphore_wait(barrier, N - 1)

    def a_copy(k):
        t = lax.rem(me + k, N)
        row, col = t // NC, lax.rem(t, NC)
        return remote(outb.at[col, row], recv.at[me], a_send.at[t], a_recv.at[me], row, col)

    @pl.loop(1, N)
    def _(k):
        a_copy(k).start()

    recv[me] = outb[c, r]

    def g_copy(t, s, k):
        a = t * NR + r
        row = lax.rem(r + k, NR)
        return remote(up.at[t, :, s, :], g.at[a, s], g_send.at[t, s, k - 1], g_recv.at[a, s], row, c)

    for t in range(TR):
        for s in range(TC):
            @pl.when(t * NR + r < s * NC + c)
            def _(t=t, s=s):
                for k in range(1, NR):
                    g_copy(t, s, k).start()

    @pl.loop(1, N)
    def _(k):
        q = lax.rem(me + k, N)
        remote(recv.at[q], recv.at[q], a_send.at[q], a_recv.at[q], r, c).wait_recv()

    def rhs_of(s):
        wanted = (s * NC + c).astype(F32)

        def body(q, total):
            x = recv[q]
            hit = x[KS:] == wanted
            data = x[:KS].reshape(KS // 8, 8, NB)
            return total + jnp.where(hit[None], data, 0.0)

        return lax.fori_loop(0, N, body, jnp.zeros((KS // 8, 8, NB), F32), unroll=8).reshape(KS, NB)

    for s in range(TC):
        acc[s] = rhs_of(jnp.int32(s))

    def y_copy(i, slot, k):
        col = lax.rem(c + k, NC)
        return remote(yall.at[i, r], yall.at[i, r], y_send.at[slot, k - 1], y_recv.at[i, r], r, col)

    def f_copy(i):
        return remote(yall.at[i, r], yall.at[i, r], f_send.at[i], y_recv.at[i, r], lax.rem(i, NR), c)

    @pl.loop(0, PB)
    def _(i):
        owner = lax.rem(i, NC)
        slot = i // NC

        @pl.when(c == owner)
        def _():
            y = dot3(acc[slot], inv[slot], 1)
            yall[i, r] = y
            sol_out[slot] = y

            @pl.loop(1, NC)
            def _(k):
                y_copy(i, slot, k).start()

        @pl.when(c != owner)
        def _():
            remote(yall.at[i, r], yall.at[i, r], f_send.at[i], y_recv.at[i, r], r, c).wait_recv()

        @pl.when(lax.rem(i, NR) != r)
        def _():
            f_copy(i).start()

        for s in range(TC):
            @pl.when(i < s * NC + c)
            def _(s=s):
                pltpu.make_async_copy(g.at[i, s], g.at[i, s], g_recv.at[i, s]).wait()
                acc[s] -= dot3(yall[i, r], g[i, s])

    for t in range(TR):
        i = t * NR + r
        for k in range(1, NR):
            p = lax.rem(r + k, NR)
            remote(yall.at[i, p], yall.at[i, p], f_send.at[i], y_recv.at[i, p], r, c).wait_recv()
        high, low = split(yall[i].reshape(NR * KS, NB))
        yh[:, t * NB:(t + 1) * NB] = high
        yl[:, t * NB:(t + 1) * NB] = low

    def p_copy(s, k):
        row = lax.rem(r + k, NR)
        return remote(part.at[s, row], rbuf.at[s, k - 1], p_send.at[s, k - 1], p_recv.at[s, k - 1], row, c)

    @pl.loop(0, TS)
    def _(s):
        pltpu.make_async_copy(uv.at[s], uv.at[s], u_sem.at[s]).wait()
        product = dot_split((yh[...], yl[...]), split(uv[s].reshape(TR * NB, NB)))
        part[s] = product.reshape(NR, KS, NB)
        for k in range(1, NR):
            p_copy(s, k).start()

    @pl.loop(0, TS)
    def _(s):
        tr_out[s] = rhs_of(TC + s) - part[s, r]

    @pl.loop(0, TS)
    def _(s):
        total = tr_out[s]
        for k in range(1, NR):
            p_copy(s, k).wait_recv()
            total = total - rbuf[s, k - 1]
        tr_out[s] = total

    @pl.loop(1, N)
    def _(k):
        a_copy(k).wait_send()

    for t in range(TR):
        for s in range(TC):
            @pl.when(t * NR + r < s * NC + c)
            def _(t=t, s=s):
                for k in range(1, NR):
                    g_copy(t, s, k).wait_send()

    for s in range(TC):
        @pl.loop(1, NC)
        def _(k, s=s):
            y_copy(s * NC + c, s, k).wait_send()

    @pl.loop(0, PB)
    def _(i):
        @pl.when(lax.rem(i, NR) != r)
        def _():
            f_copy(i).wait_send()

    @pl.loop(0, TS)
    def _(s):
        for k in range(1, NR):
            p_copy(s, k).wait_send()


def per_device(incoming, block_map, panel_row, diag_inverse):
    NR = lax.axis_size("row")
    NC = lax.axis_size("col")
    SB, NRHS, NB = incoming.shape[2:]
    KS = NRHS // NR
    TR = panel_row.shape[0]
    SLOTS = panel_row.shape[3]
    TC = diag_inverse.shape[0]
    PB = TR * NR
    TS = SLOTS - TC
    N = NR * NC
    vmem = pl.BlockSpec(memory_space=pltpu.VMEM)
    dma = pltpu.SemaphoreType.DMA
    sol, trailing = pl.pallas_call(
        functools.partial(kernel, (NR, NC, SB, KS, NB, TR, SLOTS, TC)),
        out_shape=(jax.ShapeDtypeStruct((TC, KS, NB), F32), jax.ShapeDtypeStruct((TS, KS, NB), F32)),
        in_specs=[pl.BlockSpec(memory_space=pltpu.SMEM), vmem, pl.BlockSpec(memory_space=pl.ANY), vmem],
        out_specs=(vmem, vmem),
        scratch_shapes=[
            pltpu.VMEM((NC, NR, KS + 8, NB), F32),
            pltpu.VMEM((N, KS + 8, NB), F32),
            pltpu.VMEM((PB, TC, NB, NB), F32),
            pltpu.VMEM((TS, TR, NB, NB), F32),
            pltpu.VMEM((PB, NR, KS, NB), F32),
            pltpu.VMEM((TC, KS, NB), F32),
            pltpu.VMEM((TS, NR, KS, NB), F32),
            pltpu.VMEM((TS, NR - 1, KS, NB), F32),
            pltpu.VMEM((NRHS, TR * NB), BF16),
            pltpu.VMEM((NRHS, TR * NB), BF16),
            dma((N,)),
            dma((N,)),
            dma((TR, TC, NR - 1)),
            dma((PB, TC)),
            dma((TS,)),
            dma((TC, NC - 1)),
            dma((PB, NR)),
            dma((PB,)),
            dma((TS, NR - 1)),
            dma((TS, NR - 1)),
        ],
        compiler_params=pltpu.CompilerParams(
            collective_id=0, has_side_effects=True, vmem_limit_bytes=40 * 1024 * 1024),
    )(
        block_map.reshape(SB),
        incoming.reshape(SB, NR, KS, NB),
        panel_row.reshape(TR, NB, SLOTS, NB),
        diag_inverse.reshape(TC, NB, NB),
    )
    return (
        jnp.transpose(sol, (1, 0, 2))[:, :, None, :],
        jnp.transpose(trailing, (1, 0, 2))[:, :, None, :],
    )


def solution(mesh):
    in_specs = (
        P("row", "col", None, None, None),
        P("row", "col", None),
        P(None, "row", None, None, "col", None),
        P(None, "col", None, None),
    )
    out_specs = (P("row", None, "col", None), P("row", None, "col", None))
    return jax.shard_map(
        per_device, mesh=mesh, in_specs=in_specs, out_specs=out_specs, check_vma=False
    )
```

time: 553 us -> 82.6 us (0.15)
  blocking collectives: 417 us -> 0 us
  Pallas kernels: 0 us -> 75.5 us
  waiting for transfers between devices: 69.9 us -> 0 us
  matrix products: 20.6 us -> 0 us
  between operations: 13.9 us -> 0.65 us
  local copies, waits for them, and re-layouts: 18.7 us -> 6.26 us
  starting transfers between devices: 10 us -> 0 us
    psum x16 -> x0, blocking collectives: 417 us -> none  [spread(): return lax.psum(kept, axis)]
    pallas_call x0 -> x1, Pallas kernels: none -> 75.5 us  [per_device(): pl.pallas_call(functools.partial(kernel, (NR, NC, SB, KS, NB, TR, SLOTS,...]
    reduce_scatter x1 -> x0, waiting for transfers between devices: 25.6 us -> none  [per_device(): lax.psum_scatter(jnp.einsum('tkf,tfse->kse', own_rows, local_upper[:, :,...]
    all_gather x2 -> x0, waiting for transfers between devices: 23 us -> none  [the longest x1 18.4 us: per_device(): solved = lax.all_gather(slices, 'row', axis=1, tiled=True)]
    all_to_all x2 -> x0, waiting for transfers between devices: 21.3 us -> none  [the longest x1 15.7 us: per_device(): lax.all_to_all(outgoing.reshape(grid_rows * grid_cols, rhs_share, block_s...]
    dot_general x36 -> x0, matrix products: 20.6 us -> none  [the longest x16 11.4 us: advance(): carried = jnp.einsum('jkf,jfe->ke', slices, upper_strip, precision=highest)]
    all_to_all x2 -> x0, starting transfers between devices: 9.9 us -> none  [the longest x1 7.3 us: per_device(): lax.all_to_all(labels.reshape(grid_rows * grid_cols, 1), ('row', 'col'),...]
  transfers between devices with their start and end apart: 5 -> 0, of which waited for: 5 -> 0; matrix products, arithmetic and copies ran while one was open for 2% -> 0% of each run, Pallas kernels for 0% -> 0%
where the time goes in v1:
time: 82.6 us; the launch traced here: 82.4 us
  Pallas kernels  75.5 us (91%)
  local copies, waits for them, and re-layouts  6.26 us (8%)
    pallas_call x1, Pallas kernels, per_device(): pl.pallas_call(functools.partial(kernel, (NR, NC, SB, KS, NB, TR, SLOTS,...  75.5 us
    unnamed x10, local copies, waits for them, and re-layouts  6.26 us

profile of v1, /device:TPU:0, one launch (start us, length us, event | category | flops | bytes accessed | tf_op | source)
XLA Modules:
  0.0 82.4 jit_solution(8161587559523813009)
XLA Ops:
  0.6 0.0 copy-start
  0.6 2.2 %copy-done = f32[4,1,128,16,1,128]{5,4,3,2,1,0:T(1,128)S(1)} copy-done((f32[4,1,128,16,1,128]{5,4,3,2,1,0:T(1,128)S(1)}, f32[4,1,128,16,1,128]{5,4,3,2,1,0:T(1,128)}, u32[]{:S(2)}) %copy-start) | copy-done | bytes 4194328
  2.8 0.0 copy-start.1
  2.8 0.9 %copy-done.1 = f32[1,1,4,128,128]{4,3,2,1,0:T(8,128)S(1)} copy-done((f32[1,1,4,128,128]{4,3,2,1,0:T(8,128)S(1)}, f32[1,1,4,128,128]{4,3,2,1,0:T(8,128)}, u32[]{:S(2)}) %copy-start.1) | copy-done | bytes 262168
  3.8 0.0 copy-start.2
  3.8 0.9 %copy-done.2 = f32[2,1,128,128]{3,2,1,0:T(8,128)S(1)} copy-done((f32[2,1,128,128]{3,2,1,0:T(8,128)S(1)}, f32[2,1,128,128]{3,2,1,0:T(8,128)}, u32[]{:S(2)}) %copy-start.2) | copy-done | bytes 131096
  4.7 0.0 copy-start.3
  4.7 0.7 copy-done.3
  5.3 75.5 %shard_map.59 = (f32[2,32,128]{2,1,0:T(8,128)S(1)}, f32[14,32,128]{2,1,0:T(8,128)S(1)}) custom-call(s32[4]{0:T(128)S(1)} %bitcast.15, f32[4,4,32,128]{3,2,1,0:T(8,128)S(1)} %bitcast.11, f32[4,128,16,128]{3,2,1,0:T(8,128)S(1)} %bitcast.10, f32[2,128,128]{2,1,0:T(8,128)S(1)} %bitcast.13), custom_call_target="tpu_custom_call" | custom-call | tf_op jit(solution)/shard_map/pallas_call | solution.py:234
  80.8 0.6 copy.6
  81.5 0.9 %copy.7 = f32[32,14,1,128]{3,2,1,0:T(1,128)} copy(f32[32,14,1,128]{3,0,1,2:T(8,128)S(1)} %bitcast.12) | data formatting | bytes 458752
Async XLA Ops:
  0.6 2.2 %copy-start = (f32[4,1,128,16,1,128]{5,4,3,2,1,0:T(1,128)S(1)}, f32[4,1,128,16,1,128]{5,4,3,2,1,0:T(1,128)}, u32[]{:S(2)}) copy-start(f32[4,1,128,16,1,128]{5,4,3,2,1,0:T(1,128)} %param.6) | copy-start | bytes 12582916
  2.8 0.9 %copy-start.1 = (f32[1,1,4,128,128]{4,3,2,1,0:T(8,128)S(1)}, f32[1,1,4,128,128]{4,3,2,1,0:T(8,128)}, u32[]{:S(2)}) copy-start(f32[1,1,4,128,128]{4,3,2,1,0:T(8,128)} %param.4) | copy-start | bytes 786436
  3.8 0.9 %copy-start.2 = (f32[2,1,128,128]{3,2,1,0:T(8,128)S(1)}, f32[2,1,128,128]{3,2,1,0:T(8,128)}, u32[]{:S(2)}) copy-start(f32[2,1,128,128]{3,2,1,0:T(8,128)} %param.7) | copy-start | bytes 393220
  4.7 0.7 copy-start.3

commit v2 on v1

--- a/solution.py
+++ b/solution.py
@@ -17,27 +17,28 @@
     return high, (x - high.astype(F32)).astype(BF16)
 
 
-def dot_split(a, b, b_dim=0):
-    dims = (((1,), (b_dim,)), ((), ()))
-
-    def one(x, y):
-        return lax.dot_general(x, y, dims, preferred_element_type=F32)
-
-    a_high, a_low = a
-    b_high, b_low = b
-    return one(a_high, b_high) + (one(a_low, b_high) + one(a_high, b_low))
-
-
-def dot3(a, b, b_dim=0):
-    return dot_split(split(a), split(b), b_dim)
-
-
-def kernel(sizes, bm, inc, up, inv, sol_out, tr_out, outb, recv, g, uv, yall, acc, part, rbuf, yh, yl,
-           a_send, a_recv, g_send, g_recv, u_sem, y_send, y_recv, f_send, p_send, p_recv):
+def tall(x):
+    return jnp.concatenate(split(x), axis=0)
+
+
+def wide(x):
+    return jnp.concatenate(split(x), axis=1)
+
+
+def product(a, b, b_dim=0):
+    out = lax.dot_general(a, b, (((1,), (b_dim,)), ((), ())), preferred_element_type=F32)
+    rows, cols = out.shape[0] // 2, out.shape[1] // 2
+    return out[:rows, :cols] + (out[:rows, cols:] + out[rows:, :cols])
+
+
+def kernel(sizes, bm, inc_hbm, up, inv_hbm, sol_out, tr_out, outb, recv, g, uv, yall, acc, part, rbuf, ycat, uvs,
+           inc, inv, ivs, wsp, zed,
+           a_send, a_recv, g_send, g_recv, u_sem, y_send, y_recv, f_send, p_send, p_recv, i_sem):
     NR, NC, SB, KS, NB, TR, SLOTS, TC = sizes
     PB = TR * NR
     TS = SLOTS - TC
     N = NR * NC
+    NRHS = NR * KS
     r = lax.axis_index("row")
     c = lax.axis_index("col")
     me = r * NC + c
@@ -46,6 +47,10 @@
         return pltpu.make_async_remote_copy(
             src_ref=src, dst_ref=dst, send_sem=ssem, recv_sem=rsem, device_id=(row, col), device_id_type=MESH)
 
+    inc_copy = pltpu.make_async_copy(inc_hbm, inc, i_sem.at[0])
+    inv_copy = pltpu.make_async_copy(inv_hbm, inv, i_sem.at[1])
+    inc_copy.start()
+    inv_copy.start()
     barrier = pltpu.get_barrier_semaphore()
 
     @pl.loop(1, N)
@@ -64,6 +69,8 @@
     @pl.loop(0, TS)
     def _(s):
         pltpu.make_async_copy(up.at[:, :, TC + s, :], uv.at[s], u_sem.at[s]).start()
+
+    inc_copy.wait()
 
     @pl.loop(0, NC)
     def _(cc):
@@ -102,6 +109,27 @@
                 for k in range(1, NR):
                     g_copy(t, s, k).start()
 
+    inv_copy.wait()
+    for s in range(TC):
+        ivs[s] = tall(inv[s])
+
+    @pl.loop(0, TS)
+    def _(s):
+        pltpu.make_async_copy(uv.at[s], uv.at[s], u_sem.at[s]).wait()
+        uvs[s] = wide(uv[s].reshape(TR * NB, NB))
+
+    def g_wait(i, s):
+        pltpu.make_async_copy(g.at[i, s], g.at[i, s], g_recv.at[i, s]).wait()
+
+    def prepare(s):
+        before = s * NC + c - 1
+        g_wait(before, s)
+        wsp[s] = wide(product(tall(g[before, s]), ivs[s], 1))
+
+    @pl.when(c > 0)
+    def _():
+        prepare(0)
+
     @pl.loop(1, N)
     def _(k):
         q = lax.rem(me + k, N)
@@ -118,9 +146,6 @@
 
         return lax.fori_loop(0, N, body, jnp.zeros((KS // 8, 8, NB), F32), unroll=8).reshape(KS, NB)
 
-    for s in range(TC):
-        acc[s] = rhs_of(jnp.int32(s))
-
     def y_copy(i, slot, k):
         col = lax.rem(c + k, NC)
         return remote(yall.at[i, r], yall.at[i, r], y_send.at[slot, k - 1], y_recv.at[i, r], r, col)
@@ -128,43 +153,66 @@
     def f_copy(i):
         return remote(yall.at[i, r], yall.at[i, r], f_send.at[i], y_recv.at[i, r], lax.rem(i, NR), c)
 
+    def publish(i, slot, y):
+        yall[i, r] = y
+
+        @pl.loop(1, NC)
+        def _(k):
+            y_copy(i, slot, k).start()
+
+        sol_out[slot] = y
+
+    acc[0] = rhs_of(jnp.int32(0))
+
+    @pl.when(c == 0)
+    def _():
+        publish(jnp.int32(0), 0, product(tall(acc[0]), ivs[0], 1))
+
+    @pl.when(c == 1)
+    def _():
+        zed[...] = product(tall(acc[0]), ivs[0], 1)
+
+    for s in range(1, TC):
+        acc[s] = rhs_of(jnp.int32(s))
+
     @pl.loop(0, PB)
     def _(i):
-        owner = lax.rem(i, NC)
-        slot = i // NC
-
-        @pl.when(c == owner)
-        def _():
-            y = dot3(acc[slot], inv[slot], 1)
-            yall[i, r] = y
-            sol_out[slot] = y
-
-            @pl.loop(1, NC)
-            def _(k):
-                y_copy(i, slot, k).start()
-
-        @pl.when(c != owner)
+        @pl.when(c != lax.rem(i, NC))
         def _():
             remote(yall.at[i, r], yall.at[i, r], f_send.at[i], y_recv.at[i, r], r, c).wait_recv()
+
+        y = tall(yall[i, r])
+
+        for s in range(TC):
+            @pl.when(i + 1 == s * NC + c)
+            def _(s=s):
+                publish(i + 1, s, zed[...] - product(y, wsp[s]))
 
         @pl.when(lax.rem(i, NR) != r)
         def _():
             f_copy(i).start()
 
         for s in range(TC):
-            @pl.when(i < s * NC + c)
+            @pl.when(i + 1 < s * NC + c)
             def _(s=s):
-                pltpu.make_async_copy(g.at[i, s], g.at[i, s], g_recv.at[i, s]).wait()
-                acc[s] -= dot3(yall[i, r], g[i, s])
+                g_wait(i, s)
+                acc[s] -= product(y, wide(g[i, s]))
+
+            @pl.when(i + 2 == s * NC + c)
+            def _(s=s):
+                zed[...] = product(tall(acc[s]), ivs[s], 1)
+
+            if s > 0:
+                @pl.when(i == (s - 1) * NC + c)
+                def _(s=s):
+                    prepare(s)
 
     for t in range(TR):
         i = t * NR + r
         for k in range(1, NR):
             p = lax.rem(r + k, NR)
             remote(yall.at[i, p], yall.at[i, p], f_send.at[i], y_recv.at[i, p], r, c).wait_recv()
-        high, low = split(yall[i].reshape(NR * KS, NB))
-        yh[:, t * NB:(t + 1) * NB] = high
-        yl[:, t * NB:(t + 1) * NB] = low
+        ycat[:, t * NB:(t + 1) * NB] = tall(yall[i].reshape(NRHS, NB))
 
     def p_copy(s, k):
         row = lax.rem(r + k, NR)
@@ -172,9 +220,7 @@
 
     @pl.loop(0, TS)
     def _(s):
-        pltpu.make_async_copy(uv.at[s], uv.at[s], u_sem.at[s]).wait()
-        product = dot_split((yh[...], yl[...]), split(uv[s].reshape(TR * NB, NB)))
-        part[s] = product.reshape(NR, KS, NB)
+        part[s] = product(ycat[...], uvs[s]).reshape(NR, KS, NB)
         for k in range(1, NR):
             p_copy(s, k).start()
 
@@ -234,7 +280,7 @@
     sol, trailing = pl.pallas_call(
         functools.partial(kernel, (NR, NC, SB, KS, NB, TR, SLOTS, TC)),
         out_shape=(jax.ShapeDtypeStruct((TC, KS, NB), F32), jax.ShapeDtypeStruct((TS, KS, NB), F32)),
-        in_specs=[pl.BlockSpec(memory_space=pltpu.SMEM), vmem, pl.BlockSpec(memory_space=pl.ANY), vmem],
+        in_specs=[pl.BlockSpec(memory_space=pltpu.SMEM)] + [pl.BlockSpec(memory_space=pltpu.HBM)] * 3,
         out_specs=(vmem, vmem),
         scratch_shapes=[
             pltpu.VMEM((NC, NR, KS + 8, NB), F32),
@@ -245,8 +291,13 @@
             pltpu.VMEM((TC, KS, NB), F32),
             pltpu.VMEM((TS, NR, KS, NB), F32),
             pltpu.VMEM((TS, NR - 1, KS, NB), F32),
-            pltpu.VMEM((NRHS, TR * NB), BF16),
-            pltpu.VMEM((NRHS, TR * NB), BF16),
+            pltpu.VMEM((2 * NRHS, TR * NB), BF16),
+            pltpu.VMEM((TS, TR * NB, 2 * NB), BF16),
+            pltpu.VMEM((SB, NR, KS, NB), F32),
+            pltpu.VMEM((TC, NB, NB), F32),
+            pltpu.VMEM((TC, 2 * NB, NB), BF16),
+            pltpu.VMEM((TC, NB, 2 * NB), BF16),
+            pltpu.VMEM((KS, NB), F32),
             dma((N,)),
             dma((N,)),
             dma((TR, TC, NR - 1)),
@@ -257,6 +308,7 @@
             dma((PB,)),
             dma((TS, NR - 1)),
             dma((TS, NR - 1)),
+            dma((2,)),
         ],
         compiler_params=pltpu.CompilerParams(
             collective_id=0, has_side_effects=True, vmem_limit_bytes=40 * 1024 * 1024),

time: 82.6 us -> 78.9 us (0.955)
  Pallas kernels: 75.5 us -> 71.8 us
    pallas_call x1, Pallas kernels: 75.5 us -> 71.8 us  [per_device(): pl.pallas_call(functools.partial(kernel, (NR, NC, SB, KS, NB, TR, SLOTS,...]
where the time goes in v2:
time: 78.9 us; the launch traced here: 78.7 us
  Pallas kernels  71.8 us (91%)
  local copies, waits for them, and re-layouts  6.26 us (8%)
    pallas_call x1, Pallas kernels, per_device(): pl.pallas_call(functools.partial(kernel, (NR, NC, SB, KS, NB, TR, SLOTS,...  71.8 us
    unnamed x10, local copies, waits for them, and re-layouts  6.26 us

profile of v2, /device:TPU:0, one launch (start us, length us, event | category | flops | bytes accessed | tf_op | source)
XLA Modules:
  0.0 78.7 jit_solution(1463886489966131728)
XLA Ops:
  0.6 0.0 copy-start
  0.6 2.2 %copy-done = f32[4,1,128,16,1,128]{5,4,3,2,1,0:T(1,128)S(1)} copy-done((f32[4,1,128,16,1,128]{5,4,3,2,1,0:T(1,128)S(1)}, f32[4,1,128,16,1,128]{5,4,3,2,1,0:T(1,128)}, u32[]{:S(2)}) %copy-start) | copy-done | bytes 4194328
  2.8 0.0 copy-start.1
  2.8 0.9 %copy-done.1 = f32[1,1,4,128,128]{4,3,2,1,0:T(8,128)S(1)} copy-done((f32[1,1,4,128,128]{4,3,2,1,0:T(8,128)S(1)}, f32[1,1,4,128,128]{4,3,2,1,0:T(8,128)}, u32[]{:S(2)}) %copy-start.1) | copy-done | bytes 262168
  3.8 0.0 copy-start.2
  3.8 0.9 %copy-done.2 = f32[2,1,128,128]{3,2,1,0:T(8,128)S(1)} copy-done((f32[2,1,128,128]{3,2,1,0:T(8,128)S(1)}, f32[2,1,128,128]{3,2,1,0:T(8,128)}, u32[]{:S(2)}) %copy-start.2) | copy-done | bytes 131096
  4.7 0.0 copy-start.3
  4.7 0.7 copy-done.3
  5.3 71.8 %shard_map.59 = (f32[2,32,128]{2,1,0:T(8,128)S(1)}, f32[14,32,128]{2,1,0:T(8,128)S(1)}) custom-call(s32[4]{0:T(128)S(1)} %bitcast.15, f32[4,4,32,128]{3,2,1,0:T(8,128)S(1)} %bitcast.11, f32[4,128,16,128]{3,2,1,0:T(8,128)S(1)} %bitcast.10, f32[2,128,128]{2,1,0:T(8,128)S(1)} %bitcast.13), custom_call_target="tpu_custom_call" | custom-call | tf_op jit(solution)/shard_map/pallas_call | solution.py:280
  77.1 0.6 copy.6
  77.7 0.9 %copy.7 = f32[32,14,1,128]{3,2,1,0:T(1,128)} copy(f32[32,14,1,128]{3,0,1,2:T(8,128)S(1)} %bitcast.12) | data formatting | bytes 458752
Async XLA Ops:
  0.6 2.2 %copy-start = (f32[4,1,128,16,1,128]{5,4,3,2,1,0:T(1,128)S(1)}, f32[4,1,128,16,1,128]{5,4,3,2,1,0:T(1,128)}, u32[]{:S(2)}) copy-start(f32[4,1,128,16,1,128]{5,4,3,2,1,0:T(1,128)} %param.6) | copy-start | bytes 12582916
  2.8 0.9 %copy-start.1 = (f32[1,1,4,128,128]{4,3,2,1,0:T(8,128)S(1)}, f32[1,1,4,128,128]{4,3,2,1,0:T(8,128)}, u32[]{:S(2)}) copy-start(f32[1,1,4,128,128]{4,3,2,1,0:T(8,128)} %param.4) | copy-start | bytes 786436
  3.8 0.9 %copy-start.2 = (f32[2,1,128,128]{3,2,1,0:T(8,128)S(1)}, f32[2,1,128,128]{3,2,1,0:T(8,128)}, u32[]{:S(2)}) copy-start(f32[2,1,128,128]{3,2,1,0:T(8,128)} %param.7) | copy-start | bytes 393220
  4.7 0.7 copy-start.3

commit v3 on v2

--- a/solution.py
+++ b/solution.py
@@ -32,8 +32,8 @@
 
 
 def kernel(sizes, bm, inc_hbm, up, inv_hbm, sol_out, tr_out, outb, recv, g, uv, yall, acc, part, rbuf, ycat, uvs,
-           inc, inv, ivs, wsp, zed,
-           a_send, a_recv, g_send, g_recv, u_sem, y_send, y_recv, f_send, p_send, p_recv, i_sem):
+           inc, inv, ivs, wsp, zed, row_out, row_in, blocks_out, blocks_in,
+           a_send, a_recv, g_send, g_recv, u_sem, y_send, y_recv, f_send, p_send, p_recv, i_sem, r_send, r_recv, b_send, b_recv):
     NR, NC, SB, KS, NB, TR, SLOTS, TC = sizes
     PB = TR * NR
     TS = SLOTS - TC
@@ -71,6 +71,41 @@
         pltpu.make_async_copy(up.at[:, :, TC + s, :], uv.at[s], u_sem.at[s]).start()
 
     inc_copy.wait()
+
+    for u in range(SB):
+        row_out[:, u, :KS, :] = inc[u]
+        row_out[:, u, KS:, :] = jnp.full((NR, 8, NB), bm[u].astype(F32), F32)
+    row_in[r] = row_out[r]
+
+    pl.semaphore_wait(barrier, N - 1)
+
+    def a_copy(k):
+        t = lax.rem(me + k, N)
+        row, col = t // NC, lax.rem(t, NC)
+        return remote(outb.at[col, row], recv.at[me], a_send.at[t], a_recv.at[me], row, col)
+
+    def r_copy(k):
+        row = lax.rem(r + k, NR)
+        return remote(row_out.at[row], row_in.at[r], r_send.at[k - 1], r_recv.at[r], row, c)
+
+    for k in range(1, NR):
+        r_copy(k).start()
+
+    def g_copy(t, s, k):
+        a = t * NR + r
+        row = lax.rem(r + k, NR)
+        return remote(up.at[t, :, s, :], g.at[a, s], g_send.at[t, s, k - 1], g_recv.at[a, s], row, c)
+
+    for t in range(TR):
+        for s in range(TC):
+            @pl.when(t * NR + r < s * NC + c)
+            def _(t=t, s=s):
+                for k in range(1, NR):
+                    g_copy(t, s, k).start()
+
+    inv_copy.wait()
+    for s in range(TC):
+        ivs[s] = tall(inv[s])
 
     @pl.loop(0, NC)
     def _(cc):
@@ -84,34 +119,44 @@
         outb[cc, :, :KS, :] = inc[pick]
         outb[cc, :, KS:, :] = jnp.full((NR, 8, NB), label.astype(F32), F32)
 
-    pl.semaphore_wait(barrier, N - 1)
-
-    def a_copy(k):
-        t = lax.rem(me + k, N)
-        row, col = t // NC, lax.rem(t, NC)
-        return remote(outb.at[col, row], recv.at[me], a_send.at[t], a_recv.at[me], row, col)
-
-    @pl.loop(1, N)
-    def _(k):
-        a_copy(k).start()
-
     recv[me] = outb[c, r]
 
-    def g_copy(t, s, k):
-        a = t * NR + r
+    for k in range(1, NR):
         row = lax.rem(r + k, NR)
-        return remote(up.at[t, :, s, :], g.at[a, s], g_send.at[t, s, k - 1], g_recv.at[a, s], row, c)
-
-    for t in range(TR):
-        for s in range(TC):
-            @pl.when(t * NR + r < s * NC + c)
-            def _(t=t, s=s):
-                for k in range(1, NR):
-                    g_copy(t, s, k).start()
-
-    inv_copy.wait()
-    for s in range(TC):
-        ivs[s] = tall(inv[s])
+        remote(row_in.at[row], row_in.at[row], r_send.at[k - 1], r_recv.at[row], r, c).wait_recv()
+
+    def pick(source, count, block):
+        wanted = block.astype(F32)
+
+        def body(q, total):
+            x = source(q)
+            hit = x[KS:] == wanted
+            data = x[:KS].reshape(KS // 8, 8, NB)
+            return total + jnp.where(hit[None], data, 0.0)
+
+        zeros = jnp.zeros((KS // 8, 8, NB), F32)
+        return lax.fori_loop(0, count, body, zeros, unroll=8).reshape(KS, NB)
+
+    def b_copy(s, k):
+        col = lax.rem(c + k, NC)
+        return remote(blocks_out.at[s, col], blocks_in.at[s, c], b_send.at[s, k - 1], b_recv.at[s, c], r, col)
+
+    for s in range(TC):
+        @pl.loop(1, NC)
+        def _(k, s=s):
+            col = lax.rem(c + k, NC)
+            blocks_out[s, col] = pick(lambda q: row_in[q // SB, lax.rem(q, SB)], NR * SB, s * NC + col)
+            b_copy(s, k).start()
+
+        blocks_in[s, c] = pick(lambda q: row_in[q // SB, lax.rem(q, SB)], NR * SB, s * NC + c)
+
+    def panel_rhs(s):
+        @pl.loop(1, NC)
+        def _(k):
+            q = lax.rem(c + k, NC)
+            remote(blocks_in.at[s, q], blocks_in.at[s, q], b_send.at[s, k - 1], b_recv.at[s, q], r, c).wait_recv()
+
+        return jnp.sum(blocks_in[s], axis=0)
 
     @pl.loop(0, TS)
     def _(s):
@@ -130,21 +175,8 @@
     def _():
         prepare(0)
 
-    @pl.loop(1, N)
-    def _(k):
-        q = lax.rem(me + k, N)
-        remote(recv.at[q], recv.at[q], a_send.at[q], a_recv.at[q], r, c).wait_recv()
-
     def rhs_of(s):
-        wanted = (s * NC + c).astype(F32)
-
-        def body(q, total):
-            x = recv[q]
-            hit = x[KS:] == wanted
-            data = x[:KS].reshape(KS // 8, 8, NB)
-            return total + jnp.where(hit[None], data, 0.0)
-
-        return lax.fori_loop(0, N, body, jnp.zeros((KS // 8, 8, NB), F32), unroll=8).reshape(KS, NB)
+        return pick(lambda q: recv[q], N, s * NC + c)
 
     def y_copy(i, slot, k):
         col = lax.rem(c + k, NC)
@@ -162,7 +194,7 @@
 
         sol_out[slot] = y
 
-    acc[0] = rhs_of(jnp.int32(0))
+    acc[0] = panel_rhs(0)
 
     @pl.when(c == 0)
     def _():
@@ -173,7 +205,7 @@
         zed[...] = product(tall(acc[0]), ivs[0], 1)
 
     for s in range(1, TC):
-        acc[s] = rhs_of(jnp.int32(s))
+        acc[s] = panel_rhs(s)
 
     @pl.loop(0, PB)
     def _(i):
@@ -206,6 +238,13 @@
                 @pl.when(i == (s - 1) * NC + c)
                 def _(s=s):
                     prepare(s)
+
+        for j in range(-(-N // PB)):
+            k = i * -(-N // PB) + j + 1
+
+            @pl.when(k < N)
+            def _(k=k):
+                a_copy(k).start()
 
     for t in range(TR):
         i = t * NR + r
@@ -224,6 +263,11 @@
         for k in range(1, NR):
             p_copy(s, k).start()
 
+    @pl.loop(1, N)
+    def _(k):
+        q = lax.rem(me + k, N)
+        remote(recv.at[q], recv.at[q], a_send.at[q], a_recv.at[q], r, c).wait_recv()
+
     @pl.loop(0, TS)
     def _(s):
         tr_out[s] = rhs_of(TC + s) - part[s, r]
@@ -235,6 +279,14 @@
             p_copy(s, k).wait_recv()
             total = total - rbuf[s, k - 1]
         tr_out[s] = total
+
+    for k in range(1, NR):
+        r_copy(k).wait_send()
+
+    for s in range(TC):
+        @pl.loop(1, NC)
+        def _(k, s=s):
+            b_copy(s, k).wait_send()
 
     @pl.loop(1, N)
     def _(k):
@@ -298,6 +350,10 @@
             pltpu.VMEM((TC, 2 * NB, NB), BF16),
             pltpu.VMEM((TC, NB, 2 * NB), BF16),
             pltpu.VMEM((KS, NB), F32),
+            pltpu.VMEM((NR, SB, KS + 8, NB), F32),
+            pltpu.VMEM((NR, SB, KS + 8, NB), F32),
+            pltpu.VMEM((TC, NC, KS, NB), F32),
+            pltpu.VMEM((TC, NC, KS, NB), F32),
             dma((N,)),
             dma((N,)),
             dma((TR, TC, NR - 1)),
@@ -309,9 +365,13 @@
             dma((TS, NR - 1)),
             dma((TS, NR - 1)),
             dma((2,)),
+            dma((NR - 1,)),
+            dma((NR,)),
+            dma((TC, NC - 1)),
+            dma((TC, NC)),
         ],
         compiler_params=pltpu.CompilerParams(
-            collective_id=0, has_side_effects=True, vmem_limit_bytes=40 * 1024 * 1024),
+            collective_id=0, has_side_effects=True, vmem_limit_bytes=60 * 1024 * 1024),
     )(
         block_map.reshape(SB),
         incoming.reshape(SB, NR, KS, NB),

time: 78.9 us -> 74.6 us (0.946)
  local copies, waits for them, and re-layouts: 6.26 us -> 3.27 us
  Pallas kernels: 71.8 us -> 70.4 us
    unnamed x10 -> x2, local copies, waits for them, and re-layouts: 6.26 us -> 3.27 us
    pallas_call x1, Pallas kernels: 71.8 us -> 70.4 us  [per_device(): pl.pallas_call(functools.partial(kernel, (NR, NC, SB, KS, NB, TR, SLOTS,...]
where the time goes in v3:
time: 74.6 us; the launch traced here: 74.3 us
  Pallas kernels  70.4 us (94%)
  local copies, waits for them, and re-layouts  3.27 us (4%)
    pallas_call x1, Pallas kernels, per_device(): pl.pallas_call(functools.partial(kernel, (NR, NC, SB, KS, NB, TR, SLOTS,...  70.4 us
    unnamed x2, local copies, waits for them, and re-layouts  3.27 us

profile of v3, /device:TPU:0, one launch (start us, length us, event | category | flops | bytes accessed | tf_op | source)
XLA Modules:
  0.0 74.3 jit_solution(15759444516912623346)
XLA Ops:
  0.6 70.4 %shard_map.59 = (f32[2,32,128]{2,1,0:T(8,128)}, f32[14,32,128]{2,1,0:T(8,128)}) custom-call(s32[4]{0:T(128)} %bitcast.15, f32[4,4,32,128]{3,2,1,0:T(8,128)} %bitcast.11, f32[4,128,16,128]{3,2,1,0:T(8,128)} %bitcast.10, f32[2,128,128]{2,1,0:T(8,128)} %bitcast.13), custom_call_target="tpu_custom_call" | custom-call | tf_op jit(solution)/shard_map/pallas_call | solution.py:332
  71.1 1.4 %copy.6 = f32[32,2,1,128]{3,2,1,0:T(1,128)} copy(f32[32,2,1,128]{3,0,1,2:T(8,128)} %bitcast.14) | data formatting | bytes 65536
  72.5 1.9 %copy.7 = f32[32,14,1,128]{3,2,1,0:T(1,128)} copy(f32[32,14,1,128]{3,0,1,2:T(8,128)} %bitcast.12) | data formatting | bytes 458752

commit v4 on v3

--- a/solution.py
+++ b/solution.py
@@ -41,7 +41,6 @@
     NRHS = NR * KS
     r = lax.axis_index("row")
     c = lax.axis_index("col")
-    me = r * NC + c
 
     def remote(src, dst, ssem, rsem, row, col):
         return pltpu.make_async_remote_copy(
@@ -53,10 +52,10 @@
     inv_copy.start()
     barrier = pltpu.get_barrier_semaphore()
 
-    @pl.loop(1, N)
-    def _(k):
-        t = lax.rem(me + k, N)
-        pl.semaphore_signal(barrier, inc=1, device_id=(t // NC, lax.rem(t, NC)), device_id_type=MESH)
+    for k in range(1, NR):
+        pl.semaphore_signal(barrier, inc=1, device_id=(lax.rem(r + k, NR), c), device_id_type=MESH)
+    for k in range(1, NC):
+        pl.semaphore_signal(barrier, inc=1, device_id=(r, lax.rem(c + k, NC)), device_id_type=MESH)
 
     for s in range(TC):
         for t in range(TR):
@@ -77,12 +76,15 @@
         row_out[:, u, KS:, :] = jnp.full((NR, 8, NB), bm[u].astype(F32), F32)
     row_in[r] = row_out[r]
 
-    pl.semaphore_wait(barrier, N - 1)
+    pl.semaphore_wait(barrier, NR + NC - 2)
 
     def a_copy(k):
-        t = lax.rem(me + k, N)
-        row, col = t // NC, lax.rem(t, NC)
-        return remote(outb.at[col, row], recv.at[me], a_send.at[t], a_recv.at[me], row, col)
+        col = lax.rem(c + k, NC)
+        return remote(outb.at[col], recv.at[c], a_send.at[k - 1], a_recv.at[c], r, col)
+
+    def a_wait(k):
+        q = lax.rem(c + k, NC)
+        remote(recv.at[q], recv.at[q], a_send.at[k - 1], a_recv.at[q], r, c).wait_recv()
 
     def r_copy(k):
         row = lax.rem(r + k, NR)
@@ -107,20 +109,6 @@
     for s in range(TC):
         ivs[s] = tall(inv[s])
 
-    @pl.loop(0, NC)
-    def _(cc):
-        pick = jnp.int32(0)
-        label = jnp.int32(-1)
-        for u in range(SB):
-            b = bm[u]
-            hit = lax.rem(b, NC) == cc
-            pick = jnp.where(hit, u, pick)
-            label = jnp.where(hit, b, label)
-        outb[cc, :, :KS, :] = inc[pick]
-        outb[cc, :, KS:, :] = jnp.full((NR, 8, NB), label.astype(F32), F32)
-
-    recv[me] = outb[c, r]
-
     for k in range(1, NR):
         row = lax.rem(r + k, NR)
         remote(row_in.at[row], row_in.at[row], r_send.at[k - 1], r_recv.at[row], r, c).wait_recv()
@@ -158,6 +146,23 @@
 
         return jnp.sum(blocks_in[s], axis=0)
 
+    @pl.loop(0, NC)
+    def _(cc):
+        wanted = cc.astype(F32)
+        for p in range(NR):
+            data = jnp.zeros((KS // 8, 8, NB), F32)
+            label = jnp.full((8, NB), -1.0, F32)
+            for u in range(SB):
+                x = row_in[p, u]
+                index = x[KS:]
+                hit = index - NC * jnp.floor((index + 0.5) * (1.0 / NC)) == wanted
+                data = jnp.where(hit[None], x[:KS].reshape(KS // 8, 8, NB), data)
+                label = jnp.where(hit, index, label)
+            outb[cc, p, :KS, :] = data.reshape(KS, NB)
+            outb[cc, p, KS:, :] = label
+
+    recv[c] = outb[c]
+
     @pl.loop(0, TS)
     def _(s):
         pltpu.make_async_copy(uv.at[s], uv.at[s], u_sem.at[s]).wait()
@@ -176,7 +181,7 @@
         prepare(0)
 
     def rhs_of(s):
-        return pick(lambda q: recv[q], N, s * NC + c)
+        return pick(lambda q: recv[q // NR, lax.rem(q, NR)], N, s * NC + c)
 
     def y_copy(i, slot, k):
         col = lax.rem(c + k, NC)
@@ -239,10 +244,10 @@
                 def _(s=s):
                     prepare(s)
 
-        for j in range(-(-N // PB)):
-            k = i * -(-N // PB) + j + 1
-
-            @pl.when(k < N)
+        for j in range(-(-NC // PB)):
+            k = i * -(-NC // PB) + j + 1
+
+            @pl.when(k < NC)
             def _(k=k):
                 a_copy(k).start()
 
@@ -263,10 +268,9 @@
         for k in range(1, NR):
             p_copy(s, k).start()
 
-    @pl.loop(1, N)
+    @pl.loop(1, NC)
     def _(k):
-        q = lax.rem(me + k, N)
-        remote(recv.at[q], recv.at[q], a_send.at[q], a_recv.at[q], r, c).wait_recv()
+        a_wait(k)
 
     @pl.loop(0, TS)
     def _(s):
@@ -288,7 +292,7 @@
         def _(k, s=s):
             b_copy(s, k).wait_send()
 
-    @pl.loop(1, N)
+    @pl.loop(1, NC)
     def _(k):
         a_copy(k).wait_send()
 
@@ -336,7 +340,7 @@
         out_specs=(vmem, vmem),
         scratch_shapes=[
             pltpu.VMEM((NC, NR, KS + 8, NB), F32),
-            pltpu.VMEM((N, KS + 8, NB), F32),
+            pltpu.VMEM((NC, NR, KS + 8, NB), F32),
             pltpu.VMEM((PB, TC, NB, NB), F32),
             pltpu.VMEM((TS, TR, NB, NB), F32),
             pltpu.VMEM((PB, NR, KS, NB), F32),
@@ -354,8 +358,8 @@
             pltpu.VMEM((NR, SB, KS + 8, NB), F32),
             pltpu.VMEM((TC, NC, KS, NB), F32),
             pltpu.VMEM((TC, NC, KS, NB), F32),
-            dma((N,)),
-            dma((N,)),
+            dma((NC - 1,)),
+            dma((NC,)),
             dma((TR, TC, NR - 1)),
             dma((PB, TC)),
             dma((TS,)),

time: 74.6 us -> 76.6 us (1.027)
  Pallas kernels: 70.4 us -> 72.5 us
    pallas_call x1, Pallas kernels: 70.4 us -> 72.5 us  [per_device(): pl.pallas_call(functools.partial(kernel, (NR, NC, SB, KS, NB, TR, SLOTS,...]
where the time goes in v4:
time: 76.6 us; the launch traced here: 76.4 us
  Pallas kernels  72.5 us (95%)
  local copies, waits for them, and re-layouts  3.27 us (4%)
    pallas_call x1, Pallas kernels, per_device(): pl.pallas_call(functools.partial(kernel, (NR, NC, SB, KS, NB, TR, SLOTS,...  72.5 us
    unnamed x2, local copies, waits for them, and re-layouts  3.27 us

profile of v4, /device:TPU:0, one launch (start us, length us, event | category | flops | bytes accessed | tf_op | source)
XLA Modules:
  0.0 76.4 jit_solution(4451603111827914011)
XLA Ops:
  0.6 72.5 %shard_map.59 = (f32[2,32,128]{2,1,0:T(8,128)}, f32[14,32,128]{2,1,0:T(8,128)}) custom-call(s32[4]{0:T(128)} %bitcast.15, f32[4,4,32,128]{3,2,1,0:T(8,128)} %bitcast.11, f32[4,128,16,128]{3,2,1,0:T(8,128)} %bitcast.10, f32[2,128,128]{2,1,0:T(8,128)} %bitcast.13), custom_call_target="tpu_custom_call" | custom-call | tf_op jit(solution)/shard_map/pallas_call | solution.py:336
  73.1 1.4 %copy.6 = f32[32,2,1,128]{3,2,1,0:T(1,128)} copy(f32[32,2,1,128]{3,0,1,2:T(8,128)} %bitcast.14) | data formatting | bytes 65536
  74.5 1.9 %copy.7 = f32[32,14,1,128]{3,2,1,0:T(1,128)} copy(f32[32,14,1,128]{3,0,1,2:T(8,128)} %bitcast.12) | data formatting | bytes 458752
